TPU v7x, 512 devices: a whole 4x8x8 slice. The times are simulated.
512 devices in a mesh: rep: 64 (over z, y), tp: 8 (over x, core).
Axes of the slice: x: 4, y: 8, z: 8, core: 2. Of those that a mesh axis runs over, the one named last changes fastest.
Arguments:
- suffix: bfloat16 [8192, 10240], P(('rep', 'tp')), may hold values from -5 to 5
- key_value_pages: bfloat16 [2, 384, 128, 1024], P(None, 'rep', None, 'tp'), may hold values from -5 to 5
- placement: int32 [64], replicated, may hold values from 0 to 63, each once
- lengths: int32 [64], replicated, may hold values from 1 to 384, 8192 in all
- page_table: int32 [64, 4], P('rep'), may hold values from 0 to 5, as said below
Outputs:
- attended: bfloat16 [8192, 8192], P(('rep', 'tp'))
Inputs may be any that keep to these rules, and one draw needn't show every extreme that they name: `placement`: each group holds the prefix of exactly one request. The lengths sum to 8192 and the longest is exactly 384. `page_table`: row g names 4 different pages of group g's own pool.
All inputs are finite; a program needn't handle non-finite values.
Results may differ from a plain program's by a relative error of at most 0.0046.
Values may be sent and summed in bfloat16 or wider, within the bound.
A program may use at most 64 MiB of HBM per device.

v0:
```python
import math

import jax
import jax.numpy as jnp
from jax import lax
from jax.sharding import PartitionSpec as P

QUERY_HEADS = 64
KEY_VALUE_HEADS = 8
HEAD_SIZE = 128


def attend_rows(
    work_rows, work_position, work_live, key_value_pages, page_table, heads_dev, key_heads_local
):
    row_count = work_rows.shape[0]
    group_width = QUERY_HEADS // KEY_VALUE_HEADS
    scale = 1.0 / math.sqrt(HEAD_SIZE)
    paged_rows = jnp.take(key_value_pages, page_table[0], axis=1)
    prefix_len = paged_rows.shape[1] * paged_rows.shape[2]
    prefix_keys = paged_rows[0].reshape(prefix_len, key_heads_local, HEAD_SIZE)
    prefix_vals = paged_rows[1].reshape(prefix_len, key_heads_local, HEAD_SIZE)
    row_queries = (
        work_rows[:, : heads_dev * HEAD_SIZE]
        .reshape(row_count, heads_dev, HEAD_SIZE)
        .transpose(1, 0, 2)
    )
    row_keys = work_rows[
        :, heads_dev * HEAD_SIZE : (heads_dev + key_heads_local) * HEAD_SIZE
    ].reshape(row_count, key_heads_local, HEAD_SIZE)
    row_vals = work_rows[:, (heads_dev + key_heads_local) * HEAD_SIZE :].reshape(
        row_count, key_heads_local, HEAD_SIZE
    )
    keys_all = jnp.concatenate([prefix_keys, row_keys], axis=0).transpose(1, 0, 2)
    vals_all = jnp.concatenate([prefix_vals, row_vals], axis=0).transpose(1, 0, 2)
    key_position = jnp.concatenate([jnp.full((prefix_len,), -1, jnp.int32), work_position])
    key_valid = jnp.concatenate([jnp.ones((prefix_len,), bool), work_live])
    visible = key_valid[None, :] & (key_position[None, :] <= work_position[:, None])

    def one_head(operands):
        query, head_index = operands
        kv_index = head_index // group_width
        key_block = lax.dynamic_index_in_dim(keys_all, kv_index, 0, keepdims=False)
        val_block = lax.dynamic_index_in_dim(vals_all, kv_index, 0, keepdims=False)
        scores = (
            lax.dot_general(
                query, key_block, (((1,), (1,)), ((), ())), preferred_element_type=jnp.float32
            )
            * scale
        )
        scores = jnp.where(visible, scores, -jnp.inf)
        highest = jnp.max(scores, axis=1, keepdims=True)
        expo = jnp.exp(scores - highest)
        total = jnp.sum(expo, axis=1, keepdims=True)
        weights = expo.astype(jnp.bfloat16)
        mixed = jnp.dot(weights, val_block, preferred_element_type=jnp.float32) / total
        return mixed.astype(jnp.bfloat16)

    outputs = lax.map(one_head, (row_queries, jnp.arange(heads_dev, dtype=jnp.int32)))
    return outputs.transpose(1, 0, 2).reshape(row_count, heads_dev * HEAD_SIZE)


def shards(suffix, key_value_pages, placement, lengths, page_table):
    rep_count = lax.axis_size("rep")
    tensor_parallel_count = lax.axis_size("tp")
    devices_all = rep_count * tensor_parallel_count
    rep_here = lax.axis_index("rep")
    tp_here = lax.axis_index("tp")
    device_here = rep_here * tensor_parallel_count + tp_here
    token_total = suffix.shape[0]
    heads_dev = QUERY_HEADS // tensor_parallel_count
    key_heads_local = KEY_VALUE_HEADS // tensor_parallel_count
    width_dev = (heads_dev + 2 * key_heads_local) * HEAD_SIZE
    longest = 3 * token_total * tensor_parallel_count
    most_rows = (longest + devices_all - 1) // devices_all
    ends_at = jnp.cumsum(lengths)
    starts_at = ends_at - lengths
    request_ids = jnp.arange(rep_count, dtype=jnp.int32)
    order_index = jnp.arange(token_total, dtype=jnp.int32) * devices_all + device_here
    owner_request = jnp.sum((order_index[:, None] >= ends_at[None, :]).astype(jnp.int32), axis=1)
    matches = owner_request[:, None] == request_ids[None, :]
    first_pos = jnp.sum(jnp.where(matches, starts_at[None, :], 0), axis=1)
    target_group = jnp.sum(jnp.where(matches, placement[None, :], 0), axis=1)
    slot_index = (order_index - first_pos) // devices_all
    destination = target_group * most_rows + slot_index
    query_rows = suffix[:, : QUERY_HEADS * HEAD_SIZE].reshape(
        token_total, tensor_parallel_count, heads_dev * HEAD_SIZE
    )
    suffix_key_rows = suffix[
        :, QUERY_HEADS * HEAD_SIZE : (QUERY_HEADS + KEY_VALUE_HEADS) * HEAD_SIZE
    ].reshape(token_total, tensor_parallel_count, key_heads_local * HEAD_SIZE)
    suffix_value_rows = suffix[:, (QUERY_HEADS + KEY_VALUE_HEADS) * HEAD_SIZE :].reshape(
        token_total, tensor_parallel_count, key_heads_local * HEAD_SIZE
    )
    packed = jnp.concatenate([query_rows, suffix_key_rows, suffix_value_rows], axis=2).reshape(
        token_total, tensor_parallel_count * width_dev
    )
    placing = (
        jnp.arange(rep_count * most_rows, dtype=jnp.int32)[:, None] == destination[None, :]
    ).astype(jnp.bfloat16)
    outgoing = jnp.dot(placing, packed, preferred_element_type=jnp.float32).astype(jnp.bfloat16)
    outgoing = outgoing.reshape(rep_count, most_rows, tensor_parallel_count, width_dev)
    incoming = lax.all_to_all(
        lax.all_to_all(outgoing, "rep", split_axis=0, concat_axis=0, tiled=True),
        "tp",
        split_axis=2,
        concat_axis=1,
        tiled=True,
    )
    capacity = rep_count * tensor_parallel_count * most_rows
    received = incoming.reshape(capacity, width_dev)
    slot_ids = jnp.arange(capacity, dtype=jnp.int32)
    source_rep = slot_ids // (tensor_parallel_count * most_rows)
    source_tp = slot_ids // most_rows % tensor_parallel_count
    source_slot = slot_ids % most_rows
    source_device = source_rep * tensor_parallel_count + source_tp
    here_match = placement == rep_here
    request_start = jnp.sum(jnp.where(here_match, starts_at, 0))
    request_length = jnp.sum(jnp.where(here_match, lengths, 0))
    position = source_slot * devices_all + jnp.remainder(source_device - request_start, devices_all)
    live = position < request_length
    answer_rows = attend_rows(
        received, position, live, key_value_pages, page_table, heads_dev, key_heads_local
    )
    returning = answer_rows.reshape(
        rep_count, tensor_parallel_count, most_rows, 1, heads_dev * HEAD_SIZE
    )
    came_back = lax.all_to_all(
        lax.all_to_all(returning, "rep", split_axis=0, concat_axis=0, tiled=True),
        "tp",
        split_axis=1,
        concat_axis=3,
        tiled=True,
    )
    flat_back = came_back.reshape(rep_count * most_rows, QUERY_HEADS * HEAD_SIZE)
    return jnp.dot(placing.T, flat_back, preferred_element_type=jnp.float32).astype(jnp.bfloat16)


def solution(mesh):
    return jax.shard_map(
        shards,
        mesh=mesh,
        in_specs=(P(("rep", "tp"), None), P(None, "rep", None, "tp"), P(), P(), P("rep", None)),
        out_specs=P(("rep", "tp"), None),
        check_vma=False,
    )
```

profile of v0, /device:TPU:1, one launch (start us, length us, event | category | flops | bytes accessed | tf_op | source)
XLA Modules:
  0.0 156.4 jit_solution(3886729127790320022)
XLA Ops:
  0.0 0.8 slice_bitcast_fusion.4
  0.8 1.0 slice.24
  1.8 0.7 copy.28
  3.0 1.3 fusion.28
  5.3 1.3 copy.42
  6.6 17.1 %all-to-all-start = ((bf16[64,1,8,1280]{3,2,1,0:T(8,128)(2,1)}), bf16[64,1,8,1280]{3,2,1,0:T(8,128)(2,1)S(1)}, u32[]{:S(2)}, u32[]{:S(2)}) async-start(bf16[64,1,8,1280]{3,2,1,0:T(8,128)(2,1)} %bitcast.1), calls=%async_computation | async-start | bytes 2621440 | tf_op jit(solution)/shard_map/all_to_all | solution.py:104
  23.7 33.2 %all-to-all-done = bf16[64,1,8,1280]{3,2,1,0:T(8,128)(2,1)S(1)} async-done(((bf16[64,1,8,1280]{3,2,1,0:T(8,128)(2,1)}), bf16[64,1,8,1280]{3,2,1,0:T(8,128)(2,1)S(1)}, u32[]{:S(2)}, u32[]{:S(2)}) %all-to-all-start) | async-done | bytes 1310752 | tf_op jit(solution)/shard_map/all_to_all | solution.py:104
  56.9 1.3 copy.30
  58.2 7.5 %all-to-all-start.1 = ((bf16[64,1,8,1280]{3,0,1,2:T(8,128)(2,1)}), bf16[64,1,8,1280]{3,0,1,2:T(8,128)(2,1)S(1)}, u32[]{:S(2)}, u32[]{:S(2)}) async-start(bf16[64,1,8,1280]{3,0,1,2:T(8,128)(2,1)} %copy.30), calls=%async_computation.1 | async-start | bytes 2621440 | tf_op jit(solution)/shard_map/all_to_all | solution.py:103
  65.8 0.6 gather_fusion
  66.4 1.3 broadcast_compare_fusion
  67.7 0.6 add_select_fusion
  68.4 15.2 %all-to-all-done.1 = bf16[64,1,8,1280]{3,0,1,2:T(8,128)(2,1)S(1)} async-done(((bf16[64,1,8,1280]{3,0,1,2:T(8,128)(2,1)}), bf16[64,1,8,1280]{3,0,1,2:T(8,128)(2,1)S(1)}, u32[]{:S(2)}, u32[]{:S(2)}) %all-to-all-start.1) | async-done | bytes 1310752 | tf_op jit(solution)/shard_map/all_to_all | solution.py:103
  83.6 0.7 copy.47
  84.6 14.3 %while.12 = (s32[]{:T(128)}, bf16[8,512,128]{2,1,0:T(8,128)(2,1)S(1)}, bf16[8,512,128]{2,1,0:T(8,128)(2,1)S(1)}, bf16[1,1024,128]{2,1,0:T(8,128)(2,1)S(1)}, bf16...) while((s32[]{:T(128)}, ...), condition=%wide.region_9.10_spmd.clone, body=%wide.region_6.9_spmd.clone.sunk | while | flops 273284096 | bytes 7095397 | solution.py:59
  84.6 0.7 fusion.42
  86.4 0.7 fusion.42
  88.2 0.7 fusion.42
  89.4 0.6 fusion.44
  90.0 0.7 fusion.42
  91.2 0.6 fusion.44
  91.8 0.7 fusion.42
  93.0 0.6 fusion.44
  93.6 0.7 fusion.42
  94.8 0.6 fusion.44
  95.4 0.7 fusion.42
  97.1 0.7 fusion.42
  98.9 0.7 copy.33
  100.1 33.8 %all_to_all.28 = bf16[64,8,1,1,1024]{4,1,3,2,0:T(8,128)(2,1)S(1)} all-to-all(bf16[64,8,1,1,1024]{4,1,3,2,0:T(8,128)(2,1)S(1)} %bitcast.83), channel_id=1, replica_groups=mesh['rep'=64,'tp'=8] {'rep'}, dimensions={0} | all-to-all | bytes 2097152 | tf_op jit(solution)/shard_map/all_to_all | solution.py:129
  133.9 0.6 copy.35
  134.4 20.8 %all_to_all.29 = bf16[64,8,1,1,1024]{4,0,3,2,1:T(8,128)(2,1)S(1)} all-to-all(bf16[64,8,1,1,1024]{4,0,3,2,1:T(8,128)(2,1)S(1)} %copy.35), channel_id=1, replica_groups=mesh['rep'=64,'tp'=8] {'tp'}, dimensions={1} | all-to-all | bytes 2097152 | tf_op jit(solution)/shard_map/all_to_all | solution.py:128
  155.3 1.0 convolution_convert_fusion.1
  (43 shorter events, 8.6 us)
Async XLA Ops:
  0.0 65.8 %copy-start = (bf16[2,6,128,128]{3,2,1,0:T(8,128)(2,1)S(1)}, bf16[2,6,128,128]{3,2,1,0:T(8,128)(2,1)}, u32[]{:S(2)}) copy-start(bf16[2,6,128,128]{3,2,1,0:T(8,128)(2,1)} %param.8) | copy-start | bytes 1179652
  0.0 4.6 %copy-start.1 = (s32[64]{0:T(128)S(1)}, s32[64]{0:T(128)}, u32[]{:S(2)}) copy-start(s32[64]{0:T(128)} %param.9) | copy-start | bytes 772
  6.6 50.3 %all-to-all-start = ((bf16[64,1,8,1280]{3,2,1,0:T(8,128)(2,1)}), bf16[64,1,8,1280]{3,2,1,0:T(8,128)(2,1)S(1)}, u32[]{:S(2)}, u32[]{:S(2)}) async-start(bf16[64,1,8,1280]{3,2,1,0:T(8,128)(2,1)} %bitcast.1), calls=%async_computation | async-start | bytes 2621440 | tf_op jit(solution)/shard_map/all_to_all | solution.py:104
  23.7 42.0 %copy-start.2 = (s32[1,4]{1,0:T(1,128)S(1)}, s32[1,4]{1,0:T(1,128)}, u32[]{:S(2)}) copy-start(s32[1,4]{1,0:T(1,128)} %param.11) | copy-start | bytes 52
  58.2 25.4 %all-to-all-start.1 = ((bf16[64,1,8,1280]{3,0,1,2:T(8,128)(2,1)}), bf16[64,1,8,1280]{3,0,1,2:T(8,128)(2,1)S(1)}, u32[]{:S(2)}, u32[]{:S(2)}) async-start(bf16[64,1,8,1280]{3,0,1,2:T(8,128)(2,1)} %copy.30), calls=%async_computation.1 | async-start | bytes 2621440 | tf_op jit(solution)/shard_map/all_to_all | solution.py:103
where the time goes:
time: 157 us; the launch traced here: 156 us
  blocking collectives  54.6 us (35%)
  waiting for transfers between devices  48.4 us (31%)
  starting transfers between devices  24.7 us (16%)
  matrix products  11.5 us (7%)
  local copies, waits for them, and re-layouts  8.77 us (6%)
  other arithmetic  8.14 us (5%)
    all_to_all x1, blocking collectives, shards(): lax.all_to_all(returning, 'rep', split_axis=0, concat_axis=0, tiled=True)  33.8 us
    all_to_all x1, waiting for transfers between devices, shards(): lax.all_to_all(outgoing, 'rep', split_axis=0, concat_axis=0, tiled=True)  33.2 us
    all_to_all x1, blocking collectives, shards(): lax.all_to_all(lax.all_to_all(returning, 'rep', split_axis=0, concat_axis...  20.8 us
    all_to_all x1, starting transfers between devices, shards(): lax.all_to_all(outgoing, 'rep', split_axis=0, concat_axis=0, tiled=True)  17.1 us
    all_to_all x1, waiting for transfers between devices, shards(): lax.all_to_all(lax.all_to_all(outgoing, 'rep', split_axis=0, concat_axis=...  15.2 us
    all_to_all x1, starting transfers between devices, shards(): lax.all_to_all(lax.all_to_all(outgoing, 'rep', split_axis=0, concat_axis=...  7.53 us
    dot_general x8, matrix products, one_head(): lax.dot_general(query, key_block, (((1,), (1,)), ((), ())), preferred_ele...  5.54 us
    dot_general x8, matrix products, one_head(): jnp.dot(weights, val_block, preferred_element_type=jnp.float32) / total  4.47 us
  transfers between devices with their start and end apart: 2, of which 2 were waited for; matrix products, arithmetic and copies ran while one was open for 2% of the time, Pallas kernels for 0%

commit v1 on v0

v1 whole, which is shorter than its diff:
```python
import functools
import math

import jax
import jax.numpy as jnp
from jax import lax
from jax.experimental import pallas as pl
from jax.experimental.pallas import tpu as pltpu
from jax.sharding import PartitionSpec as P

QUERY_HEADS = 64
KEY_VALUE_HEADS = 8
HEAD = 128
REPS = 64
TPS = 8
ROUNDS = 16
DEVICES = REPS * TPS
GROUP_HEADS = QUERY_HEADS // TPS
PARTS = GROUP_HEADS // 2
KV = PARTS
PREFIX = 512
BLOCK = 128
MESH = pl.DeviceIdType.MESH
F32 = jnp.float32
I32 = jnp.int32
BF16 = jnp.bfloat16


def iota(shape, dim):
    return lax.broadcasted_iota(I32, shape, dim)


def kernel(
    suffix, pages, place_row, place_col, len_row, len_col, table, out,
    rows_in, pool, pick, place, keys, vals, sent, got, ans, back, rows_out,
    pool_sem, x_send, x_recv, x_own, f_send, f_recv, f_own, b_send, b_recv, b_own, o_send, o_recv, o_own,
):
    rep = lax.axis_index("rep")
    tp = lax.axis_index("tp")
    z, y = rep // 8, lax.rem(rep, 8)

    def peer(step):
        a, b = step // 8, lax.rem(step, 8)
        return lax.rem(z + lax.rem(a + b, 8), 8) * 8 + lax.rem(y + b, 8)

    pool_copy = pltpu.make_async_copy(pages, pool, pool_sem)
    pool_copy.start()

    barrier = pltpu.get_barrier_semaphore()

    @pl.loop(1, TPS)
    def _(step):
        pl.semaphore_signal(
            barrier, inc=1, device_id=(rep, lax.rem(tp + step, TPS)), device_id_type=MESH
        )

    @pl.loop(1, REPS)
    def _(step):
        pl.semaphore_signal(barrier, inc=1, device_id=(peer(step), tp), device_id_type=MESH)

    lens_r = len_row[...].astype(F32)
    lens_c = len_col[...].astype(F32)
    square = (REPS, REPS)
    starts_r = jnp.sum(
        jnp.where(iota(square, 0) < iota(square, 1), lens_c, 0.0), axis=0, keepdims=True
    )
    starts_c = jnp.sum(
        jnp.where(iota(square, 1) < iota(square, 0), lens_r, 0.0), axis=1, keepdims=True
    )
    shape = (REPS * TPS, REPS)
    mine = place_row[...] == iota(shape, 0) // TPS
    start_g = jnp.sum(jnp.where(mine, starts_r, 0.0), axis=1, keepdims=True).astype(I32)
    shape = (REPS * TPS, TPS * ROUNDS)
    run = lax.rem(iota(shape, 0), TPS)
    round_g = (start_g - (rep * TPS + run) + (DEVICES - 1)) // DEVICES
    col = iota(shape, 1)
    pick[...] = jnp.where(
        (col // ROUNDS == run) & (lax.rem(col, ROUNDS) == round_g), 1.0, 0.0
    ).astype(BF16)
    lanes = 2 * REPS * TPS
    shape = (REPS, lanes)
    mine = place_col[...] == iota(shape, 1) // (2 * TPS)
    start_l = jnp.sum(jnp.where(mine, starts_c, 0.0), axis=0, keepdims=True).astype(I32)
    length_l = jnp.sum(jnp.where(mine, lens_c, 0.0), axis=0, keepdims=True).astype(I32)
    lane = iota((1, lanes), 1)
    order = rep * TPS + lax.rem(lane, TPS)
    round_l = (start_l - order + (DEVICES - 1)) // DEVICES
    live = round_l * DEVICES + order < start_l + length_l
    code = jnp.where(live, round_l + ROUNDS * lax.rem(lane, 2 * TPS), -1)
    shape = (2 * TPS * ROUNDS, lanes)
    place[...] = jnp.where(iota(shape, 0) == code, 1.0, 0.0).astype(BF16)
    own = place_row[...] == rep
    start = jnp.sum(jnp.where(own, starts_r, 0.0), axis=1, keepdims=True).astype(I32)
    length = jnp.sum(jnp.where(own, lens_r, 0.0), axis=1, keepdims=True).astype(I32)
    key_pos = (iota((1, DEVICES), 1) - start) & (DEVICES - 1)
    key_pos = jnp.where(key_pos < length, key_pos, DEVICES)

    pool_copy.wait()
    for i in range(PREFIX // HEAD):
        page = table[0, i]
        keys[pl.ds(i * HEAD, HEAD)] = pool[0, page]
        vals[pl.ds(i * HEAD, HEAD)] = pool[1, page]

    pl.semaphore_wait(barrier, TPS - 1 + REPS - 1)

    def x_parts(head, slot):
        wide = GROUP_HEADS * HEAD
        for source, width, to in (
            (head * wide, wide, 0),
            (QUERY_HEADS * HEAD + head * HEAD, HEAD, wide),
            ((QUERY_HEADS + KEY_VALUE_HEADS) * HEAD + head * HEAD, HEAD, wide + HEAD),
        ):
            yield (
                suffix.at[:, pl.ds(pl.multiple_of(source, HEAD), width)],
                rows_in.at[slot, :, pl.ds(to, width)],
            )

    @pl.loop(1, TPS)
    def _(step):
        to = lax.rem(tp + step, TPS)
        for source, target in x_parts(to, tp):
            pltpu.make_async_remote_copy(
                src_ref=source, dst_ref=target, send_sem=x_send, recv_sem=x_recv,
                device_id=(rep, to), device_id_type=MESH,
            ).start()

    for source, target in x_parts(tp, tp):
        pltpu.make_async_copy(source, target, x_own).start()
    others = rows_in.at[pl.ds(0, TPS - 1)]
    pltpu.make_async_copy(rows_in.at[0], rows_in.at[0], x_own).wait()
    pltpu.make_async_copy(others, others, x_recv).wait()

    def chunk(column):
        tokens = rows_in[:, :, pl.ds(column * HEAD, HEAD)].reshape(TPS * ROUNDS, HEAD)
        return jnp.dot(pick[...], tokens, preferred_element_type=F32).reshape(REPS, TPS, HEAD)

    for part in (KV, *range(PARTS)):
        sent[part] = jnp.concatenate([chunk(2 * part), chunk(2 * part + 1)], axis=1).astype(BF16)

        @pl.loop(1, REPS)
        def _(step):
            to = peer(step)
            pltpu.make_async_remote_copy(
                src_ref=sent.at[part, to], dst_ref=got.at[part, rep],
                send_sem=f_send.at[part], recv_sem=f_recv.at[part],
                device_id=(to, tp), device_id_type=MESH,
            ).start()

        pltpu.make_async_copy(sent.at[part, rep], got.at[part, rep], f_own.at[part]).start()

    def wait_part(ref, recv, local):
        pltpu.make_async_copy(ref.at[0], ref.at[0], local).wait()
        most = ref.at[pl.ds(0, REPS - 1)]
        pltpu.make_async_copy(most, most, recv).wait()

    wait_part(got.at[KV], f_recv.at[KV], f_own.at[KV])
    pair = got[KV].astype(F32)
    keys[pl.ds(PREFIX, DEVICES)] = pair[:, :TPS].reshape(DEVICES, HEAD).astype(BF16)
    vals[pl.ds(PREFIX, DEVICES)] = pair[:, TPS:].reshape(DEVICES, HEAD).astype(BF16)

    factor = math.log2(math.e) / math.sqrt(HEAD)
    tiles = BLOCK // (2 * TPS)
    for part in range(PARTS):
        wait_part(got.at[part], f_recv.at[part], f_own.at[part])

        @pl.loop(0, REPS // tiles)
        def _(step):
            first = pl.multiple_of(step * tiles, tiles)
            query = got[part, pl.ds(first, tiles)].reshape(BLOCK, HEAD)
            row = iota((BLOCK, 1), 0)
            order = (first + row // (2 * TPS)) * TPS + lax.rem(row, TPS)
            pos = (order - start) & (DEVICES - 1)
            scores = lax.dot_general(
                query, keys[...], (((1,), (1,)), ((), ())), preferred_element_type=F32
            )
            before = scores[:, :PREFIX]
            after = jnp.where(key_pos <= pos, scores[:, PREFIX:], -jnp.inf)
            highest = jnp.maximum(
                jnp.max(before, axis=1, keepdims=True), jnp.max(after, axis=1, keepdims=True)
            )
            expo_b = jnp.exp2((before - highest) * factor)
            expo_a = jnp.exp2((after - highest) * factor)
            total = jnp.sum(expo_b, axis=1, keepdims=True) + jnp.sum(expo_a, axis=1, keepdims=True)
            weights = jnp.concatenate([expo_b.astype(BF16), expo_a.astype(BF16)], axis=1)
            mixed = jnp.dot(weights, vals[...], preferred_element_type=F32) / total
            ans[part, pl.ds(first, tiles)] = mixed.astype(BF16).reshape(tiles, 2 * TPS, HEAD)

        @pl.loop(1, REPS)
        def _(step):
            to = peer(step)
            pltpu.make_async_remote_copy(
                src_ref=ans.at[part, to], dst_ref=back.at[part, rep],
                send_sem=b_send.at[part], recv_sem=b_recv.at[part],
                device_id=(to, tp), device_id_type=MESH,
            ).start()

        pltpu.make_async_copy(ans.at[part, rep], back.at[part, rep], b_own.at[part]).start()

    for part in range(PARTS):
        wait_part(back.at[part], b_recv.at[part], b_own.at[part])
        tokens = jnp.dot(
            place[...], back[part].reshape(2 * DEVICES, HEAD), preferred_element_type=F32
        ).astype(BF16).reshape(2, TPS, ROUNDS, HEAD)
        rows_out[part, :, :, pl.ds(0, HEAD)] = tokens[0]
        rows_out[part, :, :, pl.ds(HEAD, HEAD)] = tokens[1]
        column = pl.multiple_of(tp * (GROUP_HEADS * HEAD) + part * 2 * HEAD, HEAD)
        target = out.at[:, pl.ds(column, 2 * HEAD)]

        @pl.loop(1, TPS)
        def _(step):
            to = lax.rem(tp + step, TPS)
            pltpu.make_async_remote_copy(
                src_ref=rows_out.at[part, to], dst_ref=target,
                send_sem=o_send, recv_sem=o_recv,
                device_id=(rep, to), device_id_type=MESH,
            ).start()

        pltpu.make_async_copy(rows_out.at[part, tp], target, o_own).start()

    pltpu.make_async_copy(others, others, x_send).wait()
    for part in range(PARTS + 1):
        most = sent.at[part, pl.ds(0, REPS - 1)]
        pltpu.make_async_copy(most, most, f_send.at[part]).wait()
    for part in range(PARTS):
        most = ans.at[part, pl.ds(0, REPS - 1)]
        pltpu.make_async_copy(most, most, b_send.at[part]).wait()
    most = rows_out.at[:, pl.ds(0, TPS - 1)]
    pltpu.make_async_copy(most, most, o_send).wait()
    pltpu.make_async_copy(most, most, o_recv).wait()
    mine = rows_out.at[:, 0]
    pltpu.make_async_copy(mine, mine, o_own).wait()


def shards(suffix, key_value_pages, placement, lengths, page_table):
    message = (PARTS, REPS, 2 * TPS, HEAD)
    dma = pltpu.SemaphoreType.DMA
    anywhere = pl.BlockSpec(memory_space=pl.ANY)
    vmem = pl.BlockSpec(memory_space=pltpu.VMEM)
    width = (GROUP_HEADS + 2) * HEAD
    return pl.pallas_call(
        kernel,
        out_shape=jax.ShapeDtypeStruct((ROUNDS, QUERY_HEADS * HEAD), BF16),
        in_specs=[anywhere] * 2 + [vmem] * 4 + [pl.BlockSpec(memory_space=pltpu.SMEM)],
        out_specs=anywhere,
        scratch_shapes=[
            pltpu.VMEM((TPS, ROUNDS, width), BF16),
            pltpu.VMEM(key_value_pages.shape, BF16),
            pltpu.VMEM((REPS * TPS, TPS * ROUNDS), BF16),
            pltpu.VMEM((2 * TPS * ROUNDS, 2 * REPS * TPS), BF16),
            pltpu.VMEM((PREFIX + DEVICES, HEAD), BF16),
            pltpu.VMEM((PREFIX + DEVICES, HEAD), BF16),
            pltpu.VMEM((PARTS + 1, *message[1:]), BF16),
            pltpu.VMEM((PARTS + 1, *message[1:]), BF16),
            pltpu.VMEM(message, BF16),
            pltpu.VMEM(message, BF16),
            pltpu.VMEM((PARTS, TPS, ROUNDS, 2 * HEAD), BF16),
            dma, dma, dma, dma,
            dma((PARTS + 1,)), dma((PARTS + 1,)), dma((PARTS + 1,)),
            dma((PARTS,)), dma((PARTS,)), dma((PARTS,)),
            dma, dma, dma,
        ],
        compiler_params=pltpu.CompilerParams(
            collective_id=0, has_side_effects=True, vmem_limit_bytes=40 * 2**20
        ),
        cost_estimate=pl.CostEstimate(
            flops=4 * 4096 * 1024 * HEAD, bytes_accessed=2**20, transcendentals=4096 * 1024
        ),
    )(
        suffix,
        key_value_pages,
        placement.reshape(1, REPS),
        placement.reshape(REPS, 1),
        lengths.reshape(1, REPS),
        lengths.reshape(REPS, 1),
        page_table,
    )


def solution(mesh):
    return jax.shard_map(
        shards,
        mesh=mesh,
        in_specs=(P(("rep", "tp"), None), P(None, "rep", None, "tp"), P(), P(), P("rep", None)),
        out_specs=P(("rep", "tp"), None),
        check_vma=False,
    )
```

time: 157 us -> 88.8 us (0.57)
  Pallas kernels: 0 us -> 84 us
  blocking collectives: 54.6 us -> 0 us
  waiting for transfers between devices: 48.4 us -> 0 us
  starting transfers between devices: 24.7 us -> 0 us
  matrix products: 11.5 us -> 0 us
  other arithmetic: 8.14 us -> 0 us
  local copies, waits for them, and re-layouts: 8.77 us -> 4.64 us
    pallas_call x0 -> x1, Pallas kernels: none -> 84 us  [shards(): pl.pallas_call(kernel, out_shape=jax.ShapeDtypeStruct((ROUNDS, QUERY_HEAD...]
    all_to_all x2 -> x0, blocking collectives: 54.6 us -> none  [the longest x1 33.8 us: shards(): lax.all_to_all(returning, 'rep', split_axis=0, concat_axis=0, tiled=True)]
    all_to_all x2 -> x0, waiting for transfers between devices: 48.4 us -> none  [the longest x1 33.2 us: shards(): lax.all_to_all(outgoing, 'rep', split_axis=0, concat_axis=0, tiled=True)]
    all_to_all x2 -> x0, starting transfers between devices: 24.7 us -> none  [the longest x1 17.1 us: shards(): lax.all_to_all(outgoing, 'rep', split_axis=0, concat_axis=0, tiled=True)]
    dot_general x18 -> x0, matrix products: 11.5 us -> none  [the longest x8 5.54 us: one_head(): lax.dot_general(query, key_block, (((1,), (1,)), ((), ())), preferred_ele...]
    reduce_sum x11 -> x0, other arithmetic: 5.83 us -> none  [the longest x8 4.13 us: one_head(): total = jnp.sum(expo, axis=1, keepdims=True)]
    all_to_all x3 -> x0, local copies, waits for them, and re-layouts: 2.59 us -> none  [the longest x1 1.28 us: shards(): lax.all_to_all(outgoing, 'rep', split_axis=0, concat_axis=0, tiled=True)]
    unnamed x13 -> x11, local copies, waits for them, and re-layouts: 2.46 us -> 4.45 us
  transfers between devices with their start and end apart: 2 -> 0, of which waited for: 2 -> 0; matrix products, arithmetic and copies ran while one was open for 2% -> 0% of each run, Pallas kernels for 0% -> 0%
where the time goes in v1:
time: 88.8 us; the launch traced here: 88.6 us
  Pallas kernels  84 us (95%)
  local copies, waits for them, and re-layouts  4.64 us (5%)
    pallas_call x1, Pallas kernels, shards(): pl.pallas_call(kernel, out_shape=jax.ShapeDtypeStruct((ROUNDS, QUERY_HEAD...  84 us
    unnamed x11, local copies, waits for them, and re-layouts  4.45 us

profile of v1, /device:TPU:1, one launch (start us, length us, event | category | flops | bytes accessed | tf_op | source)
XLA Modules:
  0.0 88.6 jit_solution(9626449523852282563)
XLA Ops:
  0.0 0.0 copy-start.1
  0.0 0.7 copy-done.1
  0.7 0.0 copy-start
  0.7 0.1 copy.7.len_col
  0.8 0.6 copy-done
  1.3 0.0 copy-start.4
  1.3 0.1 copy.6.place_col
  1.4 0.6 copy-done.4
  2.0 0.0 copy-start.2
  2.0 1.0 %copy-done.2 = bf16[2,6,128,128]{3,2,1,0:T(8,128)(2,1)S(1)} copy-done((bf16[2,6,128,128]{3,2,1,0:T(8,128)(2,1)S(1)}, bf16[2,6,128,128]{3,2,1,0:T(8,128)(2,1)}, u32[]{:S(2)}) %copy-start.2) | copy-done | bytes 393240
  3.0 0.0 copy-start.3
  3.0 1.0 %copy-done.3 = bf16[16,10240]{1,0:T(8,128)(2,1)S(1)} copy-done((bf16[16,10240]{1,0:T(8,128)(2,1)S(1)}, bf16[16,10240]{1,0:T(8,128)(2,1)}, u32[]{:S(2)}) %copy-start.3) | copy-done | bytes 327704
  3.9 84.0 %shard_map.55 = bf16[16,8192]{1,0:T(8,128)(2,1)S(1)} custom-call(bf16[16,10240]{1,0:T(8,128)(2,1)S(1)} %copy-done.3, bf16[2,6,128,128]{3,2,1,0:T(8,128)(2,1)S(1)} %copy-done.2, s32[1,64]{1,0:T(1,128)S(1)} %bitcast.5, s32[64,1]{1,0:T(8,128)S(1)} %copy.6.place_col, s32[1,64]{1,0:T(1,128)S(1)} %bitcast.7, s32[64,1]{1,0:T(8,128)S(1)} %copy.7.len_col, ...), custom_call_target="tpu_custom_call" | custom-call | flops 2147483648 | bytes 1048576 | tf_op jit(solution)/shard_map/pallas_call | solution.py:240
  87.9 0.7 copy.9
Async XLA Ops:
  0.0 0.7 copy-start.1
  0.7 0.7 copy-start
  1.3 0.7 copy-start.4
  2.0 1.0 %copy-start.2 = (bf16[2,6,128,128]{3,2,1,0:T(8,128)(2,1)S(1)}, bf16[2,6,128,128]{3,2,1,0:T(8,128)(2,1)}, u32[]{:S(2)}) copy-start(bf16[2,6,128,128]{3,2,1,0:T(8,128)(2,1)} %pages.1) | copy-start | bytes 1179652
  3.0 1.0 %copy-start.3 = (bf16[16,10240]{1,0:T(8,128)(2,1)S(1)}, bf16[16,10240]{1,0:T(8,128)(2,1)}, u32[]{:S(2)}) copy-start(bf16[16,10240]{1,0:T(8,128)(2,1)} %suffix.1) | copy-start | bytes 983044

commit v2 on v1

v2 whole, which is shorter than its diff:
```python
import functools
import math

import jax
import jax.numpy as jnp
from jax import lax
from jax.experimental import pallas as pl
from jax.experimental.pallas import tpu as pltpu
from jax.sharding import PartitionSpec as P

QUERY_HEADS = 64
KEY_VALUE_HEADS = 8
HEAD = 128
REPS = 64
TPS = 8
ROUNDS = 16
DEVICES = REPS * TPS
GROUP_HEADS = QUERY_HEADS // TPS
PARTS = GROUP_HEADS // 2
KV = PARTS
PREFIX = 512
BLOCK = 128
MESH = pl.DeviceIdType.MESH
F32 = jnp.float32
I32 = jnp.int32
BF16 = jnp.bfloat16


def iota(shape, dim):
    return lax.broadcasted_iota(I32, shape, dim)


def one_hot(code, width):
    return jnp.where(iota((code.shape[0], width), 1) == code, 1.0, 0.0).astype(BF16)


def kernel(
    suffix, pages, placement, lengths, page_table, out,
    place_row, len_row, table, rows, heads_in, pool, pick, place, keys, vals, sent, got, pairs_out,
    ans_out, ans_in, ans, back, rows_back,
    small_sem, rows_sem, pool_sem, x_send, x_recv, x_own, k_send, k_recv, k_own, f_send, f_recv, f_own,
    a_send, a_recv, a_own, b_send, b_recv, b_own, out_sem,
):
    rep = lax.axis_index("rep")
    tp = lax.axis_index("tp")
    z, y = rep >> 3, rep & 7

    def peer(step):
        a, b = step >> 3, step & 7
        return (((z + a + b) & 7) << 3) + ((y + b) & 7)

    rows_copy = pltpu.make_async_copy(suffix, rows, rows_sem)
    rows_copy.start()
    small = [
        pltpu.make_async_copy(source, target, small_sem.at[i])
        for i, (source, target) in enumerate(
            ((placement, place_row), (lengths, len_row), (page_table, table))
        )
    ]
    for copy in small:
        copy.start()
    pool_copy = pltpu.make_async_copy(pages, pool, pool_sem)
    pool_copy.start()

    barrier = pltpu.get_barrier_semaphore()

    @pl.loop(1, REPS)
    def _(step):
        pl.semaphore_signal(barrier, inc=1, device_id=(peer(step), tp), device_id_type=MESH)

    @pl.loop(1, TPS)
    def _(step):
        pl.semaphore_signal(
            barrier, inc=1, device_id=(rep, (tp + step) & (TPS - 1)), device_id_type=MESH
        )

    def along_tp(copies, send, recv, own):
        @pl.loop(1, TPS)
        def _(step):
            to = (tp + step) & (TPS - 1)
            for source, target in copies(to):
                pltpu.make_async_remote_copy(
                    src_ref=source, dst_ref=target, send_sem=send, recv_sem=recv,
                    device_id=(rep, to), device_id_type=MESH,
                ).start()

        for source, target in copies(tp):
            pltpu.make_async_copy(source, target, own).start()

    def over_plane(source, target, send, recv, own):
        @pl.loop(1, REPS)
        def _(step):
            to = peer(step)
            pltpu.make_async_remote_copy(
                src_ref=source.at[to], dst_ref=target.at[rep], send_sem=send, recv_sem=recv,
                device_id=(to, tp), device_id_type=MESH,
            ).start()

        pltpu.make_async_copy(source.at[rep], target.at[rep], own).start()

    def wait_bytes(ref, count, sem):
        some = ref.at[pl.ds(0, count)]
        pltpu.make_async_copy(some, some, sem).wait()

    for copy in small:
        copy.wait()
    square = (REPS, REPS)
    lens_r = len_row[...].astype(F32)
    diagonal = iota(square, 0) == iota(square, 1)
    lens_c = jnp.sum(jnp.where(diagonal, lens_r, 0.0), axis=1, keepdims=True)
    starts_r = jnp.sum(
        jnp.where(iota(square, 0) < iota(square, 1), lens_c, 0.0), axis=0, keepdims=True
    )
    place_r = place_row[...]

    def round_of(start, order):
        return (start - order + (DEVICES - 1)) >> 9

    count = REPS * 2 * TPS
    row = iota((count, 1), 0)
    mine = place_r == iota((count, REPS), 0) >> 4
    start_g = jnp.sum(jnp.where(mine, starts_r, 0.0), axis=1, keepdims=True).astype(I32)
    round_g = round_of(start_g, rep * TPS + tp)
    code = jnp.where(round_g < ROUNDS, round_g + (row & (2 * TPS - 1)) * ROUNDS, -1)
    rows_copy.wait()
    pairs = jnp.concatenate(
        [rows[:, pl.ds((QUERY_HEADS + i) * HEAD, HEAD)] for i in range(2 * KEY_VALUE_HEADS)], axis=0
    )
    sent[KV] = (
        jnp.dot(one_hot(code, 2 * TPS * ROUNDS), pairs, preferred_element_type=F32)
        .astype(BF16)
        .reshape(REPS, 2 * TPS, HEAD)
    )

    pl.semaphore_wait(barrier, TPS - 1 + REPS - 1)

    def queries_along_tp(part):
        def copies(to):
            first = pl.multiple_of(to * (GROUP_HEADS * HEAD) + part * 2 * HEAD, HEAD)
            return ((rows.at[:, pl.ds(first, 2 * HEAD)], heads_in.at[part, tp]),)

        along_tp(copies, x_send.at[part], x_recv.at[part], x_own.at[part])

    queries_along_tp(0)
    over_plane(sent.at[KV], got.at[KV], f_send.at[KV], f_recv.at[KV], f_own.at[KV])
    for part in range(1, PARTS):
        queries_along_tp(part)

    run = iota((REPS * TPS, 1), 0) & (TPS - 1)
    mine = place_r == iota((REPS * TPS, REPS), 0) >> 3
    start_g = jnp.sum(jnp.where(mine, starts_r, 0.0), axis=1, keepdims=True).astype(I32)
    round_g = round_of(start_g, rep * TPS + run)
    pick[...] = one_hot(
        jnp.where(round_g < ROUNDS, round_g + run * ROUNDS, -1), TPS * ROUNDS
    )

    def chunk(part, half):
        tokens = heads_in[part, :, :, pl.ds(half * HEAD, HEAD)].reshape(TPS * ROUNDS, HEAD)
        return jnp.dot(pick[...], tokens, preferred_element_type=F32).reshape(REPS, TPS, HEAD)

    for part in range(PARTS):
        wait_bytes(heads_in.at[part], 1, x_own.at[part])
        wait_bytes(heads_in.at[part], TPS - 1, x_recv.at[part])
        sent[part] = jnp.concatenate([chunk(part, 0), chunk(part, 1)], axis=1).astype(BF16)
        over_plane(sent.at[part], got.at[part], f_send.at[part], f_recv.at[part], f_own.at[part])

    def wait_part(ref, recv, own):
        wait_bytes(ref, 1, own)
        wait_bytes(ref, REPS - 1, recv)

    turn = iota((256, 1), 0)
    turn = one_hot(((turn & 15) << 4) + (turn >> 4), 256)
    wait_part(got.at[KV], f_recv.at[KV], f_own.at[KV])
    for i in range(REPS // 16):
        block = got[KV, pl.ds(i * 16, 16)].reshape(256, HEAD)
        pairs_out[:, pl.ds(i * 16, 16)] = (
            jnp.dot(turn, block, preferred_element_type=F32).astype(BF16).reshape(16, 16, HEAD)
        )
    to_here = pl.ds(pl.multiple_of(PREFIX + tp * REPS, REPS), REPS)
    along_tp(
        lambda to: (
            (pairs_out.at[to], keys.at[to_here]),
            (pairs_out.at[TPS + to], vals.at[to_here]),
        ),
        k_send, k_recv, k_own,
    )

    place_c = jnp.sum(
        jnp.where(diagonal, place_r.astype(F32), 0.0), axis=1, keepdims=True
    ).astype(I32)
    starts_c = jnp.sum(
        jnp.where(iota(square, 1) < iota(square, 0), lens_r, 0.0), axis=1, keepdims=True
    )
    mine = place_c == iota((REPS, count), 1) >> 4
    start_l = jnp.sum(jnp.where(mine, starts_c, 0.0), axis=0, keepdims=True).astype(I32)
    length_l = jnp.sum(jnp.where(mine, lens_c, 0.0), axis=0, keepdims=True).astype(I32)
    order = rep * TPS + tp
    round_l = round_of(start_l, order)
    live = round_l * DEVICES + order < start_l + length_l
    code = round_l + ROUNDS * (iota((1, count), 1) & (2 * TPS - 1))
    shape = (2 * TPS * ROUNDS, count)
    place[...] = jnp.where(iota(shape, 0) == jnp.where(live, code, -1), 1.0, 0.0).astype(BF16)
    own = place_r == rep
    start = jnp.sum(jnp.where(own, starts_r, 0.0), axis=1, keepdims=True).astype(I32)
    length = jnp.sum(jnp.where(own, lens_r, 0.0), axis=1, keepdims=True).astype(I32)
    lane = iota((1, DEVICES), 1)
    key_pos = ((lane & (REPS - 1)) * TPS + (lane >> 6) - start) & (DEVICES - 1)
    key_pos = jnp.where(key_pos < length, key_pos, DEVICES)

    pool_copy.wait()
    for i in range(PREFIX // HEAD):
        page = table[0, i]
        keys[pl.ds(i * HEAD, HEAD)] = pool[0, page]
        vals[pl.ds(i * HEAD, HEAD)] = pool[1, page]

    wait_bytes(pairs_out, 2, k_own)
    wait_bytes(pairs_out, 2 * (TPS - 1), k_recv)

    factor = math.log2(math.e) / math.sqrt(HEAD)
    tiles = BLOCK // (2 * TPS)
    index = iota((BLOCK, 1), 0)
    by_place = one_hot((((index >> 1) & 7) << 4) + ((index & 1) << 3) + (index >> 4), BLOCK)
    by_rep = one_hot((((index >> 1) & 7) << 4) + ((index >> 4) << 1) + (index & 1), BLOCK)

    def attend(part):
        wait_part(got.at[part], f_recv.at[part], f_own.at[part])

        @pl.loop(0, REPS // tiles)
        def _(step):
            first = pl.multiple_of(step * tiles, tiles)
            query = got[part, pl.ds(first, tiles)].reshape(BLOCK, HEAD)
            order = (first + (index >> 4)) * TPS + (index & (TPS - 1))
            pos = (order - start) & (DEVICES - 1)
            scores = lax.dot_general(
                query, keys[...], (((1,), (1,)), ((), ())), preferred_element_type=F32
            )
            before = scores[:, :PREFIX]
            after = jnp.where(key_pos <= pos, scores[:, PREFIX:], -jnp.inf)
            highest = jnp.maximum(
                jnp.max(before, axis=1, keepdims=True), jnp.max(after, axis=1, keepdims=True)
            )
            expo_b = jnp.exp2((before - highest) * factor)
            expo_a = jnp.exp2((after - highest) * factor)
            total = jnp.sum(expo_b, axis=1, keepdims=True) + jnp.sum(expo_a, axis=1, keepdims=True)
            weights = jnp.concatenate([expo_b.astype(BF16), expo_a.astype(BF16)], axis=1)
            mixed = jnp.dot(weights, vals[...], preferred_element_type=F32) / total
            mixed = jnp.dot(by_place, mixed.astype(BF16), preferred_element_type=F32).astype(BF16)
            to = pl.multiple_of(step * 2 * tiles, 2 * tiles)
            ans_out[part, :, pl.ds(to, 2 * tiles)] = mixed.reshape(TPS, 2 * tiles, HEAD)

        along_tp(
            lambda to: ((ans_out.at[part, to], ans_in.at[part, tp]),),
            a_send.at[part], a_recv.at[part], a_own.at[part],
        )

    def answer(part):
        wait_bytes(ans_in.at[part], 1, a_own.at[part])
        wait_bytes(ans_in.at[part], TPS - 1, a_recv.at[part])
        for i in range(REPS // tiles):
            block = ans_in[part, :, pl.ds(i * 2 * tiles, 2 * tiles)].reshape(BLOCK, HEAD)
            ans[part, pl.ds(i * tiles, tiles)] = (
                jnp.dot(by_rep, block, preferred_element_type=F32)
                .astype(BF16)
                .reshape(tiles, 2 * TPS, HEAD)
            )
        over_plane(ans.at[part], back.at[part], b_send.at[part], b_recv.at[part], b_own.at[part])

    for part in range(PARTS):
        attend(part)
        if part > 0:
            answer(part - 1)
    answer(PARTS - 1)

    for part in range(PARTS):
        wait_part(back.at[part], b_recv.at[part], b_own.at[part])
        tokens = jnp.dot(
            place[...], back[part].reshape(count, HEAD), preferred_element_type=F32
        ).astype(BF16).reshape(TPS, 2, ROUNDS, HEAD)
        for head in range(TPS):
            for half in range(2):
                column = (head * GROUP_HEADS + 2 * part + half) * HEAD
                rows_back[:, pl.ds(column, HEAD)] = tokens[head, half]
    out_copy = pltpu.make_async_copy(rows_back, out, out_sem)
    out_copy.start()
    for part in range(PARTS):
        wait_bytes(heads_in.at[part], TPS - 1, x_send.at[part])
        wait_bytes(ans_out.at[part], TPS - 1, a_send.at[part])
        wait_bytes(ans.at[part], REPS - 1, b_send.at[part])
    for part in range(PARTS + 1):
        wait_bytes(sent.at[part], REPS - 1, f_send.at[part])
    wait_bytes(pairs_out, 2 * (TPS - 1), k_send)
    out_copy.wait()


def shards(suffix, key_value_pages, placement, lengths, page_table):
    message = (REPS, 2 * TPS, HEAD)
    dma = pltpu.SemaphoreType.DMA
    parts = dma((PARTS,))
    anywhere = pl.BlockSpec(memory_space=pltpu.HBM)
    return pl.pallas_call(
        kernel,
        out_shape=jax.ShapeDtypeStruct((ROUNDS, QUERY_HEADS * HEAD), BF16),
        in_specs=[anywhere] * 5,
        out_specs=anywhere,
        scratch_shapes=[
            pltpu.VMEM((1, REPS), I32),
            pltpu.VMEM((1, REPS), I32),
            pltpu.SMEM(page_table.shape, I32),
            pltpu.VMEM(suffix.shape, BF16),
            pltpu.VMEM((PARTS, TPS, ROUNDS, 2 * HEAD), BF16),
            pltpu.VMEM(key_value_pages.shape, BF16),
            pltpu.VMEM((REPS * TPS, TPS * ROUNDS), BF16),
            pltpu.VMEM((2 * TPS * ROUNDS, 2 * REPS * TPS), BF16),
            pltpu.VMEM((PREFIX + DEVICES, HEAD), BF16),
            pltpu.VMEM((PREFIX + DEVICES, HEAD), BF16),
            pltpu.VMEM((PARTS + 1, *message), BF16),
            pltpu.VMEM((PARTS + 1, *message), BF16),
            pltpu.VMEM((2 * TPS, REPS, HEAD), BF16),
            pltpu.VMEM((PARTS, TPS, 2 * REPS, HEAD), BF16),
            pltpu.VMEM((PARTS, TPS, 2 * REPS, HEAD), BF16),
            pltpu.VMEM((PARTS, *message), BF16),
            pltpu.VMEM((PARTS, *message), BF16),
            pltpu.VMEM((ROUNDS, QUERY_HEADS * HEAD), BF16),
            dma((3,)), dma, dma,
            parts, parts, parts,
            dma, dma, dma,
            dma((PARTS + 1,)), dma((PARTS + 1,)), dma((PARTS + 1,)),
            parts, parts, parts,
            parts, parts, parts,
            dma,
        ],
        compiler_params=pltpu.CompilerParams(
            collective_id=0, has_side_effects=True, vmem_limit_bytes=60 * 2**20
        ),
        cost_estimate=pl.CostEstimate(
            flops=4 * 4096 * 1024 * HEAD, bytes_accessed=2**20, transcendentals=4096 * 1024
        ),
    )(
        suffix,
        key_value_pages,
        placement.reshape(1, REPS),
        lengths.reshape(1, REPS),
        page_table,
    )


def solution(mesh):
    return jax.shard_map(
        shards,
        mesh=mesh,
        in_specs=(P(("rep", "tp"), None), P(None, "rep", None, "tp"), P(), P(), P("rep", None)),
        out_specs=P(("rep", "tp"), None),
        check_vma=False,
    )
```

time: 88.8 us -> 79 us (0.89)
  Pallas kernels: 84 us -> 77.1 us
  local copies, waits for them, and re-layouts: 4.64 us -> 1.67 us
    pallas_call x1, Pallas kernels: 84 us -> 77.1 us  [shards(): pl.pallas_call(kernel, out_shape=jax.ShapeDtypeStruct((ROUNDS, QUERY_HEAD...]
    unnamed x11 -> x1, local copies, waits for them, and re-layouts: 4.45 us -> 1.67 us
where the time goes in v2:
time: 79 us; the launch traced here: 78.8 us
  Pallas kernels  77.1 us (98%)
  local copies, waits for them, and re-layouts  1.67 us (2%)
    pallas_call x1, Pallas kernels, shards(): pl.pallas_call(kernel, out_shape=jax.ShapeDtypeStruct((ROUNDS, QUERY_HEAD...  77.1 us
    unnamed x1, local copies, waits for them, and re-layouts  1.67 us

profile of v2, /device:TPU:1, one launch (start us, length us, event | category | flops | bytes accessed | tf_op | source)
XLA Modules:
  0.0 78.8 jit_solution(15847098196325734463)
XLA Ops:
  0.0 77.1 %shard_map.55 = bf16[16,8192]{1,0:T(8,128)(2,1)} custom-call(bf16[16,10240]{1,0:T(8,128)(2,1)} %suffix.1, bf16[2,6,128,128]{3,2,1,0:T(8,128)(2,1)} %pages.1, s32[1,64]{1,0:T(1,128)} %bitcast.2, s32[1,64]{1,0:T(1,128)} %bitcast.3, s32[1,4]{1,0:T(1,128)} %page_table.1), custom_call_target="tpu_custom_call" | custom-call | flops 2147483648 | bytes 1048576 | tf_op jit(solution)/shard_map/pallas_call | solution.py:300
  77.2 1.7 %copy.7 = bf16[16,8192]{1,0:T(8,128)(2,1)} copy(bf16[16,8192]{1,0:T(8,128)(2,1)} %shard_map.55) | data formatting | bytes 524288

commit v3 on v2

--- a/solution.py
+++ b/solution.py
@@ -20,6 +20,8 @@
 KV = PARTS
 PREFIX = 512
 BLOCK = 128
+LONGEST = 384
+RUNS = LONGEST // TPS + 1
 MESH = pl.DeviceIdType.MESH
 F32 = jnp.float32
 I32 = jnp.int32
@@ -36,11 +38,12 @@
 
 def kernel(
     suffix, pages, placement, lengths, page_table, out,
-    place_row, len_row, table, rows, heads_in, pool, pick, place, keys, vals, sent, got, pairs_out,
+    place_row, len_row, place_s, len_s, table, rows, heads_in, pool, pick, place, keys_in, vals_in, keys, vals, sent, got_0, got_1, got_2, got_3, got_kv, pairs_out, queries, mixed,
     ans_out, ans_in, ans, back, rows_back,
     small_sem, rows_sem, pool_sem, x_send, x_recv, x_own, k_send, k_recv, k_own, f_send, f_recv, f_own,
     a_send, a_recv, a_own, b_send, b_recv, b_own, out_sem,
 ):
+    got = (got_0, got_1, got_2, got_3, got_kv)
     rep = lax.axis_index("rep")
     tp = lax.axis_index("tp")
     z, y = rep >> 3, rep & 7
@@ -54,7 +57,10 @@
     small = [
         pltpu.make_async_copy(source, target, small_sem.at[i])
         for i, (source, target) in enumerate(
-            ((placement, place_row), (lengths, len_row), (page_table, table))
+            (
+                (placement, place_row), (lengths, len_row),
+                (placement, place_s), (lengths, len_s), (page_table, table),
+            )
         )
     ]
     for copy in small:
@@ -142,7 +148,7 @@
         along_tp(copies, x_send.at[part], x_recv.at[part], x_own.at[part])
 
     queries_along_tp(0)
-    over_plane(sent.at[KV], got.at[KV], f_send.at[KV], f_recv.at[KV], f_own.at[KV])
+    over_plane(sent.at[KV], got[KV], f_send.at[KV], f_recv.at[KV], f_own.at[KV])
     for part in range(1, PARTS):
         queries_along_tp(part)
 
@@ -162,7 +168,7 @@
         wait_bytes(heads_in.at[part], 1, x_own.at[part])
         wait_bytes(heads_in.at[part], TPS - 1, x_recv.at[part])
         sent[part] = jnp.concatenate([chunk(part, 0), chunk(part, 1)], axis=1).astype(BF16)
-        over_plane(sent.at[part], got.at[part], f_send.at[part], f_recv.at[part], f_own.at[part])
+        over_plane(sent.at[part], got[part], f_send.at[part], f_recv.at[part], f_own.at[part])
 
     def wait_part(ref, recv, own):
         wait_bytes(ref, 1, own)
@@ -170,17 +176,17 @@
 
     turn = iota((256, 1), 0)
     turn = one_hot(((turn & 15) << 4) + (turn >> 4), 256)
-    wait_part(got.at[KV], f_recv.at[KV], f_own.at[KV])
+    wait_part(got[KV], f_recv.at[KV], f_own.at[KV])
     for i in range(REPS // 16):
-        block = got[KV, pl.ds(i * 16, 16)].reshape(256, HEAD)
+        block = got[KV][pl.ds(i * 16, 16)].reshape(256, HEAD)
         pairs_out[:, pl.ds(i * 16, 16)] = (
             jnp.dot(turn, block, preferred_element_type=F32).astype(BF16).reshape(16, 16, HEAD)
         )
-    to_here = pl.ds(pl.multiple_of(PREFIX + tp * REPS, REPS), REPS)
+    to_here = pl.ds(pl.multiple_of(tp * REPS, REPS), REPS)
     along_tp(
         lambda to: (
-            (pairs_out.at[to], keys.at[to_here]),
-            (pairs_out.at[TPS + to], vals.at[to_here]),
+            (pairs_out.at[to], keys_in.at[to_here]),
+            (pairs_out.at[TPS + to], vals_in.at[to_here]),
         ),
         k_send, k_recv, k_own,
     )
@@ -200,60 +206,88 @@
     code = round_l + ROUNDS * (iota((1, count), 1) & (2 * TPS - 1))
     shape = (2 * TPS * ROUNDS, count)
     place[...] = jnp.where(iota(shape, 0) == jnp.where(live, code, -1), 1.0, 0.0).astype(BF16)
-    own = place_r == rep
-    start = jnp.sum(jnp.where(own, starts_r, 0.0), axis=1, keepdims=True).astype(I32)
-    length = jnp.sum(jnp.where(own, lens_r, 0.0), axis=1, keepdims=True).astype(I32)
-    lane = iota((1, DEVICES), 1)
-    key_pos = ((lane & (REPS - 1)) * TPS + (lane >> 6) - start) & (DEVICES - 1)
-    key_pos = jnp.where(key_pos < length, key_pos, DEVICES)
+    def add(r, carry):
+        before, start = carry
+        return before + len_s[0, r], start + jnp.where(place_s[0, r] == rep, before, 0)
+
+    start = lax.fori_loop(0, REPS, add, (jnp.int32(0), jnp.int32(0)))[1]
+    length = jnp.sum(jnp.where(place_r == rep, lens_r, 0.0), axis=1, keepdims=True).astype(I32)
+    first_rep, shift = (start >> 3) & (REPS - 1), start & (TPS - 1)
+
+    factor = math.log2(math.e) / math.sqrt(HEAD)
+
+    def store_keys(first, block):
+        scaled = block.astype(F32) * factor
+        high = scaled.astype(BF16)
+        keys[pl.ds(first, block.shape[0]), pl.ds(0, HEAD)] = high
+        keys[pl.ds(first, block.shape[0]), pl.ds(HEAD, HEAD)] = (
+            scaled - high.astype(F32)
+        ).astype(BF16)
 
     pool_copy.wait()
     for i in range(PREFIX // HEAD):
         page = table[0, i]
-        keys[pl.ds(i * HEAD, HEAD)] = pool[0, page]
+        store_keys(i * HEAD, pool[0, page])
         vals[pl.ds(i * HEAD, HEAD)] = pool[1, page]
-
+    mixed[...] = jnp.zeros_like(mixed)
+
+    lane = iota((1, DEVICES), 1)
+    pos = ((lane & (REPS - 1)) * TPS + (lane >> 6) - start) & (DEVICES - 1)
+    pos = jnp.where(pos < length, pos, DEVICES)
+    in_order = jnp.where(iota((LONGEST, DEVICES), 0) == pos, 1.0, 0.0).astype(BF16)
     wait_bytes(pairs_out, 2, k_own)
     wait_bytes(pairs_out, 2 * (TPS - 1), k_recv)
-
-    factor = math.log2(math.e) / math.sqrt(HEAD)
+    store_keys(PREFIX, jnp.dot(in_order, keys_in[...], preferred_element_type=F32))
+    vals[pl.ds(PREFIX, LONGEST)] = jnp.dot(
+        in_order, vals_in[...], preferred_element_type=F32
+    ).astype(BF16)
+
     tiles = BLOCK // (2 * TPS)
     index = iota((BLOCK, 1), 0)
     by_place = one_hot((((index >> 1) & 7) << 4) + ((index & 1) << 3) + (index >> 4), BLOCK)
     by_rep = one_hot((((index >> 1) & 7) << 4) + ((index >> 4) << 1) + (index & 1), BLOCK)
 
+    def attend_runs(first, count, reach):
+        height = count * 2 * TPS
+        query = queries[pl.ds(first, count)].reshape(height, HEAD)
+        row = iota((height, 1), 0)
+        pos = (first + (row >> 4)) * TPS + (row & (TPS - 1)) - shift
+        width = PREFIX + reach
+        scores = lax.dot_general(
+            jnp.concatenate([query, query], axis=1), keys[pl.ds(0, width)],
+            (((1,), (1,)), ((), ())), preferred_element_type=F32,
+        )
+        seen = PREFIX + max(0, (first * TPS - TPS) // HEAD * HEAD)
+        column = iota((1, width - seen), 1) + (seen - PREFIX)
+        after = jnp.where(column <= pos, scores[:, seen:], -jnp.inf)
+        scores = jnp.concatenate([scores[:, :seen], after], axis=1)
+        expo = jnp.exp2(scores - jnp.max(scores, axis=1, keepdims=True))
+        total = jnp.sum(expo, axis=1, keepdims=True)
+        result = jnp.dot(expo.astype(BF16), vals[pl.ds(0, width)], preferred_element_type=F32)
+        mixed[pl.ds(first, count)] = (result / total).astype(BF16).reshape(count, 2 * TPS, HEAD)
+
+    def arrive(part):
+        wait_part(got[part], f_recv.at[part], f_own.at[part])
+
     def attend(part):
-        wait_part(got.at[part], f_recv.at[part], f_own.at[part])
-
-        @pl.loop(0, REPS // tiles)
-        def _(step):
-            first = pl.multiple_of(step * tiles, tiles)
-            query = got[part, pl.ds(first, tiles)].reshape(BLOCK, HEAD)
-            order = (first + (index >> 4)) * TPS + (index & (TPS - 1))
-            pos = (order - start) & (DEVICES - 1)
-            scores = lax.dot_general(
-                query, keys[...], (((1,), (1,)), ((), ())), preferred_element_type=F32
+        for run in range(RUNS):
+            queries[run] = got[part][(first_rep + run) & (REPS - 1)]
+        step = HEAD // TPS
+        for i in range(LONGEST // HEAD):
+            last = i == LONGEST // HEAD - 1
+            attend_runs(i * step, step + (RUNS - LONGEST // TPS if last else 0), (i + 1) * HEAD)
+        for i in range(REPS // tiles):
+            block = [mixed[(i * tiles + m - first_rep) & (REPS - 1)] for m in range(tiles)]
+            block = jnp.dot(by_place, jnp.concatenate(block, axis=0), preferred_element_type=F32)
+            ans_out[part, :, pl.ds(i * 2 * tiles, 2 * tiles)] = block.astype(BF16).reshape(
+                TPS, 2 * tiles, HEAD
             )
-            before = scores[:, :PREFIX]
-            after = jnp.where(key_pos <= pos, scores[:, PREFIX:], -jnp.inf)
-            highest = jnp.maximum(
-                jnp.max(before, axis=1, keepdims=True), jnp.max(after, axis=1, keepdims=True)
-            )
-            expo_b = jnp.exp2((before - highest) * factor)
-            expo_a = jnp.exp2((after - highest) * factor)
-            total = jnp.sum(expo_b, axis=1, keepdims=True) + jnp.sum(expo_a, axis=1, keepdims=True)
-            weights = jnp.concatenate([expo_b.astype(BF16), expo_a.astype(BF16)], axis=1)
-            mixed = jnp.dot(weights, vals[...], preferred_element_type=F32) / total
-            mixed = jnp.dot(by_place, mixed.astype(BF16), preferred_element_type=F32).astype(BF16)
-            to = pl.multiple_of(step * 2 * tiles, 2 * tiles)
-            ans_out[part, :, pl.ds(to, 2 * tiles)] = mixed.reshape(TPS, 2 * tiles, HEAD)
-
         along_tp(
             lambda to: ((ans_out.at[part, to], ans_in.at[part, tp]),),
             a_send.at[part], a_recv.at[part], a_own.at[part],
         )
 
-    def answer(part):
+    def prepare(part):
         wait_bytes(ans_in.at[part], 1, a_own.at[part])
         wait_bytes(ans_in.at[part], TPS - 1, a_recv.at[part])
         for i in range(REPS // tiles):
@@ -263,13 +297,26 @@
                 .astype(BF16)
                 .reshape(tiles, 2 * TPS, HEAD)
             )
+
+    def answer(part):
         over_plane(ans.at[part], back.at[part], b_send.at[part], b_recv.at[part], b_own.at[part])
 
-    for part in range(PARTS):
-        attend(part)
-        if part > 0:
-            answer(part - 1)
-    answer(PARTS - 1)
+    arrive(0)
+    attend(0)
+    arrive(1)
+    attend(1)
+    prepare(0)
+    answer(0)
+    arrive(2)
+    attend(2)
+    prepare(1)
+    answer(1)
+    arrive(3)
+    attend(3)
+    prepare(2)
+    answer(2)
+    prepare(3)
+    answer(3)
 
     for part in range(PARTS):
         wait_part(back.at[part], b_recv.at[part], b_own.at[part])
@@ -305,23 +352,29 @@
         scratch_shapes=[
             pltpu.VMEM((1, REPS), I32),
             pltpu.VMEM((1, REPS), I32),
+            pltpu.SMEM((1, REPS), I32),
+            pltpu.SMEM((1, REPS), I32),
             pltpu.SMEM(page_table.shape, I32),
             pltpu.VMEM(suffix.shape, BF16),
             pltpu.VMEM((PARTS, TPS, ROUNDS, 2 * HEAD), BF16),
             pltpu.VMEM(key_value_pages.shape, BF16),
             pltpu.VMEM((REPS * TPS, TPS * ROUNDS), BF16),
             pltpu.VMEM((2 * TPS * ROUNDS, 2 * REPS * TPS), BF16),
-            pltpu.VMEM((PREFIX + DEVICES, HEAD), BF16),
-            pltpu.VMEM((PREFIX + DEVICES, HEAD), BF16),
+            pltpu.VMEM((DEVICES, HEAD), BF16),
+            pltpu.VMEM((DEVICES, HEAD), BF16),
+            pltpu.VMEM((PREFIX + LONGEST, 2 * HEAD), BF16),
+            pltpu.VMEM((PREFIX + LONGEST, HEAD), BF16),
             pltpu.VMEM((PARTS + 1, *message), BF16),
-            pltpu.VMEM((PARTS + 1, *message), BF16),
+            *[pltpu.VMEM(message, BF16)] * (PARTS + 1),
             pltpu.VMEM((2 * TPS, REPS, HEAD), BF16),
+            pltpu.VMEM((RUNS, 2 * TPS, HEAD), BF16),
+            pltpu.VMEM(message, BF16),
             pltpu.VMEM((PARTS, TPS, 2 * REPS, HEAD), BF16),
             pltpu.VMEM((PARTS, TPS, 2 * REPS, HEAD), BF16),
             pltpu.VMEM((PARTS, *message), BF16),
             pltpu.VMEM((PARTS, *message), BF16),
             pltpu.VMEM((ROUNDS, QUERY_HEADS * HEAD), BF16),
-            dma((3,)), dma, dma,
+            dma((5,)), dma, dma,
             parts, parts, parts,
             dma, dma, dma,
             dma((PARTS + 1,)), dma((PARTS + 1,)), dma((PARTS + 1,)),

time: 79 us -> 75.2 us (0.952)
  Pallas kernels: 77.1 us -> 73.4 us
    pallas_call x1, Pallas kernels: 77.1 us -> 73.4 us  [shards(): pl.pallas_call(kernel, out_shape=jax.ShapeDtypeStruct((ROUNDS, QUERY_HEAD...]
where the time goes in v3:
time: 75.2 us; the launch traced here: 75.1 us
  Pallas kernels  73.4 us (98%)
  local copies, waits for them, and re-layouts  1.67 us (2%)
    pallas_call x1, Pallas kernels, shards(): pl.pallas_call(kernel, out_shape=jax.ShapeDtypeStruct((ROUNDS, QUERY_HEAD...  73.4 us
    unnamed x1, local copies, waits for them, and re-layouts  1.67 us

profile of v3, /device:TPU:1, one launch (start us, length us, event | category | flops | bytes accessed | tf_op | source)
XLA Modules:
  0.0 75.1 jit_solution(10652736687238344643)
XLA Ops:
  0.0 73.4 %shard_map.55 = bf16[16,8192]{1,0:T(8,128)(2,1)} custom-call(bf16[16,10240]{1,0:T(8,128)(2,1)} %suffix.1, bf16[2,6,128,128]{3,2,1,0:T(8,128)(2,1)} %pages.1, s32[1,64]{1,0:T(1,128)} %bitcast.2, s32[1,64]{1,0:T(1,128)} %bitcast.3, s32[1,4]{1,0:T(1,128)} %page_table.1), custom_call_target="tpu_custom_call" | custom-call | flops 2147483648 | bytes 1048576 | tf_op jit(solution)/shard_map/pallas_call | solution.py:347
  73.4 1.7 %copy.7 = bf16[16,8192]{1,0:T(8,128)(2,1)} copy(bf16[16,8192]{1,0:T(8,128)(2,1)} %shard_map.55) | data formatting | bytes 524288

commit v4 on v3

--- a/solution.py
+++ b/solution.py
@@ -50,7 +50,7 @@
 
     def peer(step):
         a, b = step >> 3, step & 7
-        return (((z + a + b) & 7) << 3) + ((y + b) & 7)
+        return (((z + b) & 7) << 3) + ((y + a + b) & 7)
 
     rows_copy = pltpu.make_async_copy(suffix, rows, rows_sem)
     rows_copy.start()
@@ -343,7 +343,7 @@
     message = (REPS, 2 * TPS, HEAD)
     dma = pltpu.SemaphoreType.DMA
     parts = dma((PARTS,))
-    anywhere = pl.BlockSpec(memory_space=pltpu.HBM)
+    anywhere = pl.BlockSpec(memory_space=pl.ANY)
     return pl.pallas_call(
         kernel,
         out_shape=jax.ShapeDtypeStruct((ROUNDS, QUERY_HEADS * HEAD), BF16),
@@ -383,7 +383,7 @@
             dma,
         ],
         compiler_params=pltpu.CompilerParams(
-            collective_id=0, has_side_effects=True, vmem_limit_bytes=60 * 2**20
+            collective_id=0, has_side_effects=True, vmem_limit_bytes=56_100_000
         ),
         cost_estimate=pl.CostEstimate(
             flops=4 * 4096 * 1024 * HEAD, bytes_accessed=2**20, transcendentals=4096 * 1024

time: 75.2 us -> 73.1 us (0.972)
  Pallas kernels: 73.4 us -> 71.5 us
    pallas_call x1, Pallas kernels: 73.4 us -> 71.5 us  [shards(): pl.pallas_call(kernel, out_shape=jax.ShapeDtypeStruct((ROUNDS, QUERY_HEAD...]
    unnamed x1 -> x7, local copies, waits for them, and re-layouts: 1.67 us -> 1.39 us
where the time goes in v4:
time: 73.1 us; the launch traced here: 72.9 us
  Pallas kernels  71.5 us (98%)
  local copies, waits for them, and re-layouts  1.39 us (2%)
    pallas_call x1, Pallas kernels, shards(): pl.pallas_call(kernel, out_shape=jax.ShapeDtypeStruct((ROUNDS, QUERY_HEAD...  71.5 us

profile of v4, /device:TPU:1, one launch (start us, length us, event | category | flops | bytes accessed | tf_op | source)
XLA Modules:
  0.0 72.9 jit_solution(16079697508933444470)
XLA Ops:
  0.0 0.0 copy-start
  0.0 0.0 copy-start.1
  0.0 0.0 copy-start.2
  0.0 0.6 copy-done
  0.7 0.0 copy-done.1
  0.7 0.0 copy-done.2
  0.7 71.5 %shard_map.55 = bf16[16,8192]{1,0:T(8,128)(2,1)S(1)} custom-call(bf16[16,10240]{1,0:T(8,128)(2,1)} %suffix.1, bf16[2,6,128,128]{3,2,1,0:T(8,128)(2,1)} %pages.1, s32[1,64]{1,0:T(1,128)S(1)} %bitcast.2, s32[1,64]{1,0:T(1,128)S(1)} %bitcast.3, s32[1,4]{1,0:T(1,128)S(1)} %copy-done.2), custom_call_target="tpu_custom_call" | custom-call | flops 2147483648 | bytes 1048576 | tf_op jit(solution)/shard_map/pallas_call | solution.py:347
  72.2 0.7 copy.7
Async XLA Ops:
  0.0 0.7 copy-start
  0.0 0.7 copy-start.1
  0.0 0.7 copy-start.2

commit v5 on v4

--- a/solution.py
+++ b/solution.py
@@ -39,9 +39,9 @@
 def kernel(
     suffix, pages, placement, lengths, page_table, out,
     place_row, len_row, place_s, len_s, table, rows, heads_in, pool, pick, place, keys_in, vals_in, keys, vals, sent, got_0, got_1, got_2, got_3, got_kv, pairs_out, queries, mixed,
-    ans_out, ans_in, ans, back, rows_back,
+    ans_out, ans_in, ans, back,
     small_sem, rows_sem, pool_sem, x_send, x_recv, x_own, k_send, k_recv, k_own, f_send, f_recv, f_own,
-    a_send, a_recv, a_own, b_send, b_recv, b_own, out_sem,
+    a_send, a_recv, a_own, b_send, b_recv, b_own,
 ):
     got = (got_0, got_1, got_2, got_3, got_kv)
     rep = lax.axis_index("rep")
@@ -50,7 +50,7 @@
 
     def peer(step):
         a, b = step >> 3, step & 7
-        return (((z + b) & 7) << 3) + ((y + a + b) & 7)
+        return (((z + b) & 7) << 3) + ((y + a + 3 * b) & 7)
 
     rows_copy = pltpu.make_async_copy(suffix, rows, rows_sem)
     rows_copy.start()
@@ -326,9 +326,7 @@
         for head in range(TPS):
             for half in range(2):
                 column = (head * GROUP_HEADS + 2 * part + half) * HEAD
-                rows_back[:, pl.ds(column, HEAD)] = tokens[head, half]
-    out_copy = pltpu.make_async_copy(rows_back, out, out_sem)
-    out_copy.start()
+                out[:, pl.ds(column, HEAD)] = tokens[head, half]
     for part in range(PARTS):
         wait_bytes(heads_in.at[part], TPS - 1, x_send.at[part])
         wait_bytes(ans_out.at[part], TPS - 1, a_send.at[part])
@@ -336,7 +334,6 @@
     for part in range(PARTS + 1):
         wait_bytes(sent.at[part], REPS - 1, f_send.at[part])
     wait_bytes(pairs_out, 2 * (TPS - 1), k_send)
-    out_copy.wait()
 
 
 def shards(suffix, key_value_pages, placement, lengths, page_table):
@@ -348,7 +345,7 @@
         kernel,
         out_shape=jax.ShapeDtypeStruct((ROUNDS, QUERY_HEADS * HEAD), BF16),
         in_specs=[anywhere] * 5,
-        out_specs=anywhere,
+        out_specs=pl.BlockSpec(memory_space=pltpu.VMEM),
         scratch_shapes=[
             pltpu.VMEM((1, REPS), I32),
             pltpu.VMEM((1, REPS), I32),
@@ -373,14 +370,12 @@
             pltpu.VMEM((PARTS, TPS, 2 * REPS, HEAD), BF16),
             pltpu.VMEM((PARTS, *message), BF16),
             pltpu.VMEM((PARTS, *message), BF16),
-            pltpu.VMEM((ROUNDS, QUERY_HEADS * HEAD), BF16),
             dma((5,)), dma, dma,
             parts, parts, parts,
             dma, dma, dma,
             dma((PARTS + 1,)), dma((PARTS + 1,)), dma((PARTS + 1,)),
             parts, parts, parts,
             parts, parts, parts,
-            dma,
         ],
         compiler_params=pltpu.CompilerParams(
             collective_id=0, has_side_effects=True, vmem_limit_bytes=56_100_000

time: 73.1 us -> 72.7 us (level)
  no operation moved by 1% of the time
where the time goes in v5:
time: 72.7 us; the launch traced here: 72.6 us
  Pallas kernels  71.2 us (98%)
  local copies, waits for them, and re-layouts  1.39 us (2%)
    pallas_call x1, Pallas kernels, shards(): pl.pallas_call(kernel, out_shape=jax.ShapeDtypeStruct((ROUNDS, QUERY_HEAD...  71.2 us

profile of v5, /device:TPU:1, one launch (start us, length us, event | category | flops | bytes accessed | tf_op | source)
XLA Modules:
  0.0 72.6 jit_solution(6845248163461565249)
XLA Ops:
  0.0 0.0 copy-start
  0.0 0.0 copy-start.1
  0.0 0.0 copy-start.2
  0.0 0.6 copy-done
  0.7 0.0 copy-done.1
  0.7 0.0 copy-done.2
  0.7 71.2 %shard_map.55 = bf16[16,8192]{1,0:T(8,128)(2,1)S(1)} custom-call(bf16[16,10240]{1,0:T(8,128)(2,1)} %suffix.1, bf16[2,6,128,128]{3,2,1,0:T(8,128)(2,1)} %pages.1, s32[1,64]{1,0:T(1,128)S(1)} %bitcast.2, s32[1,64]{1,0:T(1,128)S(1)} %bitcast.3, s32[1,4]{1,0:T(1,128)S(1)} %copy-done.2), custom_call_target="tpu_custom_call" | custom-call | flops 2147483648 | bytes 1048576 | tf_op jit(solution)/shard_map/pallas_call | solution.py:344
  71.9 0.7 copy.7
Async XLA Ops:
  0.0 0.7 copy-start
  0.0 0.7 copy-start.1
  0.0 0.7 copy-start.2

commit v6 on v5

--- a/solution.py
+++ b/solution.py
@@ -52,6 +52,18 @@
         a, b = step >> 3, step & 7
         return (((z + b) & 7) << 3) + ((y + a + 3 * b) & 7)
 
+    barrier = pltpu.get_barrier_semaphore()
+
+    @pl.loop(1, REPS, unroll=REPS - 1)
+    def _(step):
+        pl.semaphore_signal(barrier, inc=1, device_id=(peer(step), tp), device_id_type=MESH)
+
+    @pl.loop(1, TPS, unroll=TPS - 1)
+    def _(step):
+        pl.semaphore_signal(
+            barrier, inc=1, device_id=(rep, (tp + step) & (TPS - 1)), device_id_type=MESH
+        )
+
     rows_copy = pltpu.make_async_copy(suffix, rows, rows_sem)
     rows_copy.start()
     small = [
@@ -67,18 +79,6 @@
         copy.start()
     pool_copy = pltpu.make_async_copy(pages, pool, pool_sem)
     pool_copy.start()
-
-    barrier = pltpu.get_barrier_semaphore()
-
-    @pl.loop(1, REPS)
-    def _(step):
-        pl.semaphore_signal(barrier, inc=1, device_id=(peer(step), tp), device_id_type=MESH)
-
-    @pl.loop(1, TPS)
-    def _(step):
-        pl.semaphore_signal(
-            barrier, inc=1, device_id=(rep, (tp + step) & (TPS - 1)), device_id_type=MESH
-        )
 
     def along_tp(copies, send, recv, own):
         @pl.loop(1, TPS)

time: 72.7 us -> 72.6 us (level)
  no operation moved by 1% of the time
where the time goes in v6:
time: 72.6 us; the launch traced here: 72.5 us
  Pallas kernels  71.1 us (98%)
  local copies, waits for them, and re-layouts  1.39 us (2%)
    pallas_call x1, Pallas kernels, shards(): pl.pallas_call(kernel, out_shape=jax.ShapeDtypeStruct((ROUNDS, QUERY_HEAD...  71.1 us

profile of v6, /device:TPU:1, one launch (start us, length us, event | category | flops | bytes accessed | tf_op | source)
XLA Modules:
  0.0 72.5 jit_solution(13181906787944485380)
XLA Ops:
  0.0 0.0 copy-start
  0.0 0.0 copy-start.1
  0.0 0.0 copy-start.2
  0.0 0.6 copy-done
  0.7 0.0 copy-done.1
  0.7 0.0 copy-done.2
  0.7 71.1 %shard_map.55 = bf16[16,8192]{1,0:T(8,128)(2,1)S(1)} custom-call(bf16[16,10240]{1,0:T(8,128)(2,1)} %suffix.1, bf16[2,6,128,128]{3,2,1,0:T(8,128)(2,1)} %pages.1, s32[1,64]{1,0:T(1,128)S(1)} %bitcast.2, s32[1,64]{1,0:T(1,128)S(1)} %bitcast.3, s32[1,4]{1,0:T(1,128)S(1)} %copy-done.2), custom_call_target="tpu_custom_call" | custom-call | flops 2147483648 | bytes 1048576 | tf_op jit(solution)/shard_map/pallas_call | solution.py:344
  71.8 0.7 copy.7
Async XLA Ops:
  0.0 0.7 copy-start
  0.0 0.7 copy-start.1
  0.0 0.7 copy-start.2
